TPU v7x, 32 devices: a whole 2x2x4 slice. The times are simulated.
32 devices in a mesh: groups: 2 (over y), blk: 4 (over z), sub: 2 (over x), lev: 2 (over core).
Axes of the slice: x: 2, y: 2, z: 4, core: 2. Of those that a mesh axis runs over, the one named last changes fastest.
Arguments:
- ocean_forcing: float32 [4, 512, 4, 8, 128], P(('groups', 'sub'), 'blk'), parts along dimension 0, may hold values from -6 to 6
- ice_home: int32 [4, 512], P(('groups', 'sub'), 'blk'), parts along dimension 0, may hold values from -1 to 383, as said below
- ice_velocity: float32 [4, 384, 2, 8, 128], P(('groups', 'sub'), 'blk'), parts along dimension 0, may hold values from -3 to 3
- ice_stress: float32 [4, 384, 3, 8, 128], P(('groups', 'sub'), 'blk'), parts along dimension 0, may hold values from -3 to 3
- ice_area: float32 [4, 384, 4, 8, 128], P(('groups', 'sub'), 'blk', 'lev'), parts along dimension 0, may hold values from 0 to 0.24
- ice_thick: float32 [4, 384, 4, 8, 128], P(('groups', 'sub'), 'blk', 'lev'), parts along dimension 0, may hold values from 0.2 to 4
- neighbors: int32 [4, 384, 6], P(('groups', 'sub'), 'blk'), parts along dimension 0, may hold values from -1 to 767, as said below
Outputs:
- ocean_stress: float32 [4, 512, 2, 8, 128], P(('groups', 'sub'), 'blk'), parts along dimension 0
- final_velocity: float32 [4, 384, 2, 8, 128], P(('groups', 'sub'), 'blk'), parts along dimension 0
- final_stress: float32 [4, 384, 3, 8, 128], P(('groups', 'sub'), 'blk'), parts along dimension 0
There are 2 independent parts, one for each index of `groups`. A program takes and returns all parts, laid end to end along the dimension named above; each array names one. Nothing has to cross between parts.
Inputs may be any that keep to these rules, and one draw needn't show every extreme that they name: `ice_home`: sector q holds the block columns q * 4 to q * 4 + 3 of the grid; its block b lies in block row b // 4, column b % 4. The blocks with ice of a sector, numbered k = 0, 1, ... in block order, are dealt in runs of 4: run r = k // 4 lies in pass p = r // 4 at place m = r % 4, and goes to owner m along blk in even passes and 3 - m in odd ones, slot p * 4 + k % 4; the entry is owner * 96 + slot; -1 marks a block without ice. Each sector has exactly 384 blocks with ice, all in its first 97 block rows. `neighbors`: entry d of an ice block names the ice block beside it: d = 0 the next block row, 1 the next block column, 2 the previous row, 3 the previous column, 4 the previous row and next column, 5 the next row and previous column (columns run on across sectors), as (o * 2 + q) * 96 + s for owner o, sector q, slot s; -1 where that block has no ice or lies outside the grid. A named block's owner differs from the block's own by at most one along blk, and its sector by at most one. The last slot of the last owner in the last sector is always named by some entry.
All inputs are finite; a program needn't handle non-finite values.
Results may differ from a plain program's by a relative error of at most 0.0003.
Values sent between devices are 32-bit elements; how exact they have to be, the bound alone decides.
A program may use at most 128 MiB of HBM per device.

v0:
```python
import functools

import jax
import jax.numpy as jnp
from jax import lax
from jax.experimental import pallas as pl
from jax.experimental.pallas import tpu as pltpu
from jax.sharding import PartitionSpec as P

SCOLS = 4
ITERS = 4
UNROLL = 4

strength_scale = 4.0
cover_decay = 4.0
elastic_weight = 1.0
ellipse_square = 4.0
delta_floor = 0.05
inertia = 2.0
speed_floor = 0.2
coriolis = 0.6

MESH = pl.DeviceIdType.MESH


def kernel(
    owners,
    sectors,
    src_ref,
    lane_ref,
    row_ref,
    beside_ref,
    ocean_ref,
    vel_in,
    stress_in,
    area_in,
    thick_in,
    ocean_out,
    vel,
    sig,
    send_buf,
    edge_send,
    forcing,
    edge_land,
    cover,
    area_buf,
    mass_buf,
    strength_buf,
    blend,
    back,
    vel_sec,
    vel_cross,
    str_sec,
    str_cross,
    pick_vel,
    pick_str,
    out_send,
    out_recv,
    edge_sems,
    fwd_send,
    fwd_recv,
    cover_sems,
    halo_send,
    halo_recv,
    ret_send,
    ret_recv,
    ret_edge,
    back_send,
    back_recv,
):
    group = lax.axis_index("groups")
    me = lax.axis_index("blk")
    sector = lax.axis_index("sub")
    lev = lax.axis_index("lev")
    slots = vel.shape[0]
    blocks = ocean_ref.shape[0]
    cap = blocks // owners
    chunks = slots // cap
    section = vel_sec.shape[0] // 4
    f32 = jnp.float32

    def at(blk, sub=None, core=None):
        return (
            group,
            blk,
            sector if sub is None else sub,
            lev if core is None else core,
        )

    partner = at(me, None, 1 - lev)

    def remote(src, dst, send, recv, target):
        return pltpu.make_async_remote_copy(
            src_ref=src,
            dst_ref=dst,
            send_sem=send,
            recv_sem=recv,
            device_id=target,
            device_id_type=MESH,
        )

    lanes = lax.broadcasted_iota(jnp.int32, (8, 128), 1)
    subs = lax.broadcasted_iota(jnp.int32, (8, 128), 0)
    zero = jnp.zeros((8, 128), f32)

    for sec in (vel_sec, str_sec):
        for a in range(3):
            sec[a * section + 2 * slots : (a + 1) * section, :] = jnp.zeros((16, 128), f32)
        sec[3 * section :, :] = jnp.zeros((section, 128), f32)
    vel_cross[...] = jnp.zeros_like(vel_cross)
    str_cross[...] = jnp.zeros_like(str_cross)

    barrier = pltpu.get_barrier_semaphore()

    def greet(target):
        pl.semaphore_signal(barrier, inc=1, device_id=target, device_id_type=MESH)

    greet(partner)
    for delta in range(1, owners):
        greet(at(lax.rem(me + delta, owners)))
    expected = owners
    for ds in (-1, 1):
        for da in (-1, 0, 1):
            q, o = sector + ds, me + da
            ok = (q >= 0) & (q < sectors) & (o >= 0) & (o < owners)

            @pl.when(ok)
            def _():
                greet(at(o, q))

            expected = expected + ok.astype(jnp.int32)
    pl.semaphore_wait(barrier, expected)

    def out_copy(o, s):
        return remote(
            send_buf.at[o],
            forcing.at[lev, pl.ds(s * cap, cap)],
            out_send.at[o],
            out_recv.at[s],
            at(o),
        )

    full = me * cap < slots
    for delta in list(range(1, owners)):
        o = lax.rem(me + delta, owners)

        @pl.when(full)
        def _():
            def fill(j, c):
                src = src_ref[o * cap + j]
                safe = jnp.maximum(src, 0)
                for f in range(2):
                    tile = ocean_ref[safe, 2 * lev + f]
                    send_buf[o, j, f] = jnp.where(src >= 0, tile, 0.0)
                return c

            lax.fori_loop(0, cap, fill, 0, unroll=UNROLL)
            out_copy(o, me).start()

    def edge_owner(s):
        last_pass = s * (cap // SCOLS) - 1
        return jnp.where(lax.rem(last_pass + 2, 2) == 0, owners - 1, 0)

    def has_edge(s):
        return (s >= 1) & (s <= chunks)

    def edge_copy(s, o):
        return remote(
            edge_send, edge_land.at[s], edge_sems.at[0], edge_sems.at[1 + s], at(o)
        )

    @pl.when(has_edge(me))
    def _():
        for j in range(SCOLS):
            src = src_ref[blocks + j]
            safe = jnp.maximum(src, 0)
            for f in range(4):
                edge_send[j, f] = jnp.where(src >= 0, ocean_ref[safe, f], 0.0)
        edge_copy(me, edge_owner(me)).start()

    def halo_copies(sec, cross, down, base):
        mine = sec.at[pl.ds(section, section)]
        cols = sec.at[pl.ds(section + 2 * slots, 16)]
        made = []
        made.append((me + 1 < owners, remote(
            mine, sec.at[pl.ds(0, section)], halo_send.at[base], halo_recv.at[base],
            at(me + 1)), me >= 1))
        made.append((me >= 1, remote(
            mine, sec.at[pl.ds(2 * section, section)], halo_send.at[base + 1],
            halo_recv.at[base + 1], at(me - 1)), me + 1 < owners))
        target = sector + down
        source = sector - down
        t_ok = (target >= 0) & (target < sectors)
        s_ok = (source >= 0) & (source < sectors)
        for i, da in enumerate((1, 0, -1)):
            o, p = me + da, me - da
            made.append((t_ok & (o >= 0) & (o < owners), remote(
                cols, cross.at[1 - da], halo_send.at[base + 2 + i],
                halo_recv.at[base + 2 + i], at(o, target)),
                s_ok & (p >= 0) & (p < owners)))
        return made

    vel_halo = halo_copies(vel_sec, vel_cross, -1, 0)
    str_halo = halo_copies(str_sec, str_cross, 1, 5)

    def halo_start(copies):
        for ok, copy, _ in copies:
            pl.when(ok)(copy.start)

    def halo_wait(copies):
        for ok, copy, arriving in copies:
            pl.when(arriving)(copy.wait_recv)
            pl.when(ok)(copy.wait_send)

    def pack(sec, j, row_a, row_b):
        sec[pl.ds(section + j, 1), :] = row_a
        sec[pl.ds(section + slots + j, 1), :] = row_b

    def put_cols(sec, cols):
        sec[section + 2 * slots : section + 2 * slots + 8, :] = cols[0]
        sec[section + 2 * slots + 8 : section + 2 * slots + 16, :] = cols[1]

    def pack_velocity(j, cols, x, y):
        pack(vel_sec, j, x[0:1], y[0:1])
        here = lanes == j
        return (
            jnp.where(here, x[:, 0:1], cols[0]),
            jnp.where(here, y[:, 0:1], cols[1]),
        )

    def start_body(j, cols):
        x, y = vel_in[j, 0], vel_in[j, 1]
        vel[j, 0] = x
        vel[j, 1] = y
        return pack_velocity(j, cols, x, y)

    cols = lax.fori_loop(0, slots, start_body, (zero, zero), unroll=UNROLL)
    put_cols(vel_sec, cols)
    halo_start(vel_halo)

    def part_body(j, c):
        first, second = area_in[j, 0], area_in[j, 1]
        cover[0, 0, j] = first + second
        cover[0, 1, j] = first * thick_in[j, 0] + second * thick_in[j, 1]
        return c

    lax.fori_loop(0, slots, part_body, 0, unroll=UNROLL)
    cover_copy = remote(
        cover.at[0], cover.at[1], cover_sems.at[0], cover_sems.at[1], partner
    )
    cover_copy.start()

    @pl.when(full)
    def _():
        def fill(j, c):
            src = src_ref[me * cap + j]
            safe = jnp.maximum(src, 0)
            for f in range(4):
                tile = ocean_ref[safe, f]
                forcing[f // 2, me * cap + j, f % 2] = jnp.where(src >= 0, tile, 0.0)
            return c

        lax.fori_loop(0, cap, fill, 0, unroll=UNROLL)

    spot = lax.broadcasted_iota(jnp.int32, (128, 128), 0)
    for beside, d, toward in ((pick_vel, 1, 1), (pick_str, 3, -1)):
        ids = beside_ref[d : d + 1, :]
        for i in range(6):
            across, aside = i % 3 - 1, (i // 3) * toward
            base = ((me + across) * sectors + sector + aside) * slots
            hit = (ids - base == spot) & (spot < slots) & (ids >= 0)
            beside[i * 128 : (i + 1) * 128, :] = hit.astype(f32).astype(jnp.bfloat16)

    def fetch_columns(sec, cross, pick):
        parts = [
            sec[a * section + 2 * slots : (a + 1) * section, :] for a in range(3)
        ] + [cross[a] for a in range(3)]
        whole = jnp.concatenate(parts, axis=1)
        first = whole.astype(jnp.bfloat16)
        rest = whole - first.astype(f32)
        second = rest.astype(jnp.bfloat16)
        third = (rest - second.astype(f32)).astype(jnp.bfloat16)
        terms = jnp.concatenate([first, second, third], axis=0)
        got = jnp.dot(terms, pick[...], preferred_element_type=f32)
        got = got[0:16] + got[16:32] + got[32:48]
        return got[0:8], got[8:16]

    cover_copy.wait()

    def cover_body(j, c):
        area = cover[0, 0, j] + cover[1, 0, j]
        volume = cover[0, 1, j] + cover[1, 1, j]
        area_buf[j] = area
        mass_buf[j] = volume
        strength_buf[j] = strength_scale * volume * jnp.exp(-cover_decay * (1.0 - area))
        return c

    lax.fori_loop(0, slots, cover_body, 0, unroll=UNROLL)

    def fwd_copy(s, half):
        place = forcing.at[half, pl.ds(s * cap, cap)]
        return remote(place, place, fwd_send.at[s], fwd_recv.at[s], partner)

    def ret_copy(s, o):
        return remote(
            blend.at[lev, pl.ds(s * cap, cap)],
            back.at[lev, pl.ds(o * cap, cap)],
            ret_send.at[s],
            ret_recv.at[o],
            at(s),
        )

    def ret_edge_copy(s):
        return remote(
            blend.at[:, pl.ds(s * cap - SCOLS, SCOLS)],
            back.at[:, pl.ds(blocks, SCOLS)],
            ret_edge.at[1 + s],
            ret_edge.at[0],
            at(s),
        )

    for sweep in range(ITERS):
        source = stress_in if sweep == 0 else sig
        halo_wait(vel_halo)
        right_x, right_y = fetch_columns(vel_sec, vel_cross, pick_vel)

        def stress_body(j, cols):
            x, y = vel[j, 0], vel[j, 1]
            place = row_ref[j]
            below_x = vel_sec[pl.ds(place, 1), :]
            below_y = vel_sec[pl.ds(place + slots, 1), :]
            last_row, last_col = subs == 7, lanes == 127
            next_x_of_x = jnp.where(last_row, below_x, pltpu.roll(x, 7, 0))
            next_x_of_y = jnp.where(last_row, below_y, pltpu.roll(y, 7, 0))
            turn = 127 - j
            next_y_of_x = jnp.where(last_col, pltpu.roll(right_x, turn, 1), pltpu.roll(x, 127, 1))
            next_y_of_y = jnp.where(last_col, pltpu.roll(right_y, turn, 1), pltpu.roll(y, 127, 1))
            strength = strength_buf[j]
            stretch_x = next_x_of_x - x
            stretch_y = next_y_of_y - y
            shear_rate = next_y_of_x - x + (next_x_of_y - y)
            divergence = stretch_x + stretch_y
            tension = stretch_x - stretch_y
            square = (
                divergence * divergence
                + (tension * tension + shear_rate * shear_rate) * (1.0 / ellipse_square)
                + delta_floor * delta_floor
            )
            weight = elastic_weight * strength * lax.rsqrt(square)
            relax = 1.0 / (1.0 + elastic_weight)
            one = (source[j, 0] + weight * divergence - elastic_weight * strength) * relax
            two = (source[j, 1] + weight * tension * (1.0 / ellipse_square)) * relax
            shear = (source[j, 2] + weight * shear_rate * (0.5 / ellipse_square)) * relax
            sig[j, 0] = one
            sig[j, 1] = two
            sig[j, 2] = shear
            normal_x = 0.5 * (one + two)
            normal_y = 0.5 * (one - two)
            pack(str_sec, j, normal_x[7:8], shear[7:8])
            here = lanes == j
            return (
                jnp.where(here, shear[:, 127:128], cols[0]),
                jnp.where(here, normal_y[:, 127:128], cols[1]),
            )

        cols = lax.fori_loop(0, slots, stress_body, (zero, zero), unroll=UNROLL)
        put_cols(str_sec, cols)
        halo_start(str_halo)
        halo_wait(str_halo)
        left_shear, left_normal = fetch_columns(str_sec, str_cross, pick_str)

        final = sweep == ITERS - 1

        def flow_body(j, cols):
            x, y = vel[j, 0], vel[j, 1]
            one, two, shear = sig[j, 0], sig[j, 1], sig[j, 2]
            normal_x = 0.5 * (one + two)
            normal_y = 0.5 * (one - two)
            place = row_ref[slots + j]
            above_n = str_sec[pl.ds(place, 1), :]
            above_s = str_sec[pl.ds(place + slots, 1), :]
            first_row, first_col = subs == 0, lanes == 0
            turn = 128 - j
            turn = jnp.where(turn == 128, 0, turn)
            above_normal = jnp.where(first_row, above_n, pltpu.roll(normal_x, 1, 0))
            above_shear = jnp.where(first_row, above_s, pltpu.roll(shear, 1, 0))
            before_shear = jnp.where(
                first_col, pltpu.roll(left_shear, turn, 1), pltpu.roll(shear, 1, 1)
            )
            before_normal = jnp.where(
                first_col, pltpu.roll(left_normal, turn, 1), pltpu.roll(normal_y, 1, 1)
            )
            force_x = normal_x - above_normal + (shear - before_shear)
            force_y = shear - above_shear + (normal_y - before_normal)
            wind_x, wind_y = forcing[0, j, 0], forcing[0, j, 1]
            cur_x, cur_y = forcing[1, j, 0], forcing[1, j, 1]
            slip_x, slip_y = cur_x - x, cur_y - y
            drag = jnp.sqrt(slip_x * slip_x + slip_y * slip_y + speed_floor * speed_floor)
            mass = mass_buf[j]
            heavy = mass * inertia
            diagonal = heavy + drag
            rotation = mass * coriolis
            rhs_x = heavy * x + force_x + wind_x + drag * cur_x
            rhs_y = heavy * y + force_y + wind_y + drag * cur_y
            inverse = 1.0 / (diagonal * diagonal + rotation * rotation)
            x = (diagonal * rhs_x + rotation * rhs_y) * inverse
            y = (diagonal * rhs_y - rotation * rhs_x) * inverse
            vel[j, 0] = x
            vel[j, 1] = y
            if not final:
                return pack_velocity(j, cols, x, y)
            slip_x, slip_y = cur_x - x, cur_y - y
            drag = jnp.sqrt(slip_x * slip_x + slip_y * slip_y + speed_floor * speed_floor)
            area = area_buf[j]
            blend[0, j] = area * drag * slip_x + (1.0 - area) * wind_x
            blend[1, j] = area * drag * slip_y + (1.0 - area) * wind_y
            return cols

        cols = (zero, zero)
        if sweep == 0:
            for s in range(chunks):

                @pl.when(me != s)
                def _():
                    out_copy(0, s).wait_recv()
                    fwd_copy(s, lev).start()

            for s in range(chunks):

                @pl.when(me != s)
                def _():
                    fwd_copy(s, 1 - lev).wait_recv()
                    fwd_copy(s, lev).wait_send()

            for s in range(1, chunks + 1):

                @pl.when(me == edge_owner(s))
                def _():
                    edge_copy(s, me).wait_recv()
                    for j in range(SCOLS):
                        for f in range(4):
                            spot_j = s * cap - SCOLS + j
                            forcing[f // 2, spot_j, f % 2] += edge_land[s, j, f]

        if final:
            for s in range(chunks):
                lax.fori_loop(s * cap, (s + 1) * cap, flow_body, cols, unroll=UNROLL)

                @pl.when(me != s)
                def _():
                    ret_copy(s, me).start()

            for s in range(1, chunks + 1):

                @pl.when(me == edge_owner(s))
                def _():
                    ret_edge_copy(s).start()

        else:
            cols = lax.fori_loop(0, slots, flow_body, cols, unroll=UNROLL)
            put_cols(vel_sec, cols)
            halo_start(vel_halo)

    @pl.when(full)
    def _():
        def keep(j, c):
            for f in range(2):
                back[f, me * cap + j] = blend[f, me * cap + j]
            return c

        lax.fori_loop(0, cap, keep, 0, unroll=UNROLL)

    def back_copy(o, half):
        place = back.at[half, pl.ds(o * cap, cap)]
        return remote(place, place, back_send.at[o], back_recv.at[o], partner)

    @pl.when(full)
    def _():
        for delta in range(1, owners):
            o = lax.rem(me + delta, owners)
            ret_copy(0, o).wait_recv()
            back_copy(o, lev).start()
        for delta in range(1, owners):
            o = lax.rem(me + delta, owners)
            back_copy(o, 1 - lev).wait_recv()
            back_copy(o, lev).wait_send()

    @pl.when(has_edge(me))
    def _():
        ret_edge_copy(me).wait_recv()
        edge_copy(me, edge_owner(me)).wait_send()

    @pl.when(full)
    def _():
        for delta in range(1, owners):
            out_copy(lax.rem(me + delta, owners), me).wait_send()

    for s in range(chunks):

        @pl.when(me != s)
        def _():
            ret_copy(s, me).wait_send()

    for s in range(1, chunks + 1):

        @pl.when(me == edge_owner(s))
        def _():
            ret_edge_copy(s).wait_send()

    def ocean_body(b, c):
        lane = lane_ref[b]
        safe = jnp.maximum(lane, 0)
        for f in range(2):
            ocean_out[b, f] = jnp.where(lane >= 0, back[f, safe], ocean_ref[b, f])
        return c

    lax.fori_loop(0, blocks, ocean_body, 0, unroll=UNROLL)


def on_device(ocean_forcing, ice_home, ice_velocity, ice_stress, ice_area, ice_thick, neighbors):
    owners = lax.axis_size("blk")
    sectors = lax.axis_size("sub")
    me = lax.axis_index("blk")
    sector = lax.axis_index("sub")
    home = ice_home[0]
    table = neighbors[0]
    blocks = ocean_forcing.shape[1]
    slots = ice_velocity.shape[1]
    cap = blocks // owners
    chunks = slots // cap
    section = 2 * slots + 16

    present = home >= 0
    position = home % slots - me * cap
    lane = jnp.where(position >= 0, home // slots * cap + position, blocks + SCOLS + position)
    lane = jnp.where(present, lane, -1)
    wanted = jnp.arange(blocks + SCOLS, dtype=jnp.int32)
    ids = jnp.arange(blocks, dtype=jnp.int32)
    src = jnp.max(jnp.where(wanted[:, None] == lane[None, :], ids[None, :], -1), axis=1)

    beside = table.T
    rows = jnp.stack([beside[0], beside[2]])
    across = rows // slots // sectors - me + 1
    rows_at = jnp.where(rows >= 0, jnp.clip(across, 0, 2) * section + rows % slots, 3 * section)
    beside = jnp.pad(beside, ((0, 2), (0, 128 - slots)), constant_values=-1)

    f32 = jnp.float32
    tile = ocean_forcing.shape[3:]
    vmem = pl.BlockSpec(memory_space=pltpu.VMEM)
    smem = pl.BlockSpec(memory_space=pltpu.SMEM)
    dma = pltpu.SemaphoreType.DMA
    outs = pl.pallas_call(
        functools.partial(kernel, owners, sectors),
        out_shape=(
            jax.ShapeDtypeStruct((blocks, 2) + tile, f32),
            jax.ShapeDtypeStruct((slots, 2) + tile, f32),
            jax.ShapeDtypeStruct((slots, 3) + tile, f32),
        ),
        in_specs=[smem] * 3 + [vmem] * 6,
        out_specs=(vmem,) * 3,
        scratch_shapes=[
            pltpu.VMEM((owners, cap, 2) + tile, f32),
            pltpu.VMEM((SCOLS, 4) + tile, f32),
            pltpu.VMEM((2, slots, 2) + tile, f32),
            pltpu.VMEM((chunks + 1, SCOLS, 4) + tile, f32),
            pltpu.VMEM((2, 2, slots) + tile, f32),
            pltpu.VMEM((slots,) + tile, f32),
            pltpu.VMEM((slots,) + tile, f32),
            pltpu.VMEM((slots,) + tile, f32),
            pltpu.VMEM((2, slots) + tile, f32),
            pltpu.VMEM((2, blocks + SCOLS) + tile, f32),
            pltpu.VMEM((4 * section, 128), f32),
            pltpu.VMEM((3, 16, 128), f32),
            pltpu.VMEM((4 * section, 128), f32),
            pltpu.VMEM((3, 16, 128), f32),
            pltpu.VMEM((6 * 128, 128), jnp.bfloat16),
            pltpu.VMEM((6 * 128, 128), jnp.bfloat16),
            dma((owners,)),
            dma((owners,)),
            dma((chunks + 2,)),
            dma((chunks,)),
            dma((chunks,)),
            dma((2,)),
            dma((10,)),
            dma((10,)),
            dma((chunks,)),
            dma((owners,)),
            dma((chunks + 2,)),
            dma((owners,)),
            dma((owners,)),
        ],
        compiler_params=pltpu.CompilerParams(
            collective_id=0, has_side_effects=True, vmem_limit_bytes=48 * 2**20
        ),
    )(
        src,
        lane,
        rows_at.reshape(2 * slots),
        beside,
        ocean_forcing[0],
        ice_velocity[0],
        ice_stress[0],
        ice_area[0],
        ice_thick[0],
    )
    return tuple(out[None] for out in outs)


def solution(mesh):
    return jax.shard_map(
        on_device,
        mesh=mesh,
        in_specs=(
            P(("groups", "sub"), "blk", None, None, None),
            P(("groups", "sub"), "blk"),
            P(("groups", "sub"), "blk", None, None, None),
            P(("groups", "sub"), "blk", None, None, None),
            P(("groups", "sub"), "blk", "lev", None, None),
            P(("groups", "sub"), "blk", "lev", None, None),
            P(("groups", "sub"), "blk", None),
        ),
        out_specs=(
            P(("groups", "sub"), "blk", None, None, None),
            P(("groups", "sub"), "blk", None, None, None),
            P(("groups", "sub"), "blk", None, None, None),
        ),
        check_vma=False,
    )
```

profile of v0, /device:TPU:0, one launch (start us, length us, event | category | flops | bytes accessed | tf_op | source)
XLA Modules:
  0.0 117.8 jit_solution(6886391835753408116)
XLA Ops:
  0.6 0.7 fusion.3
  1.3 0.7 bitcast_select_fusion.lane_ref
  2.0 0.1 select_reduce_fusion.src_ref
  2.1 0.7 copy.12
  2.8 0.1 ne.75
  2.9 0.1 ge.31
  3.0 0.1 div.31
  3.1 0.1 rem.58
  3.2 0.0 copy-start
  3.2 1.1 copy-done
  4.3 0.0 copy-start.1
  4.3 1.1 copy-done.1
  5.5 0.0 copy-start.2
  5.5 1.1 copy-done.2
  6.6 108.3 %shard_map.94 = (f32[128,2,8,128]{3,2,1,0:T(8,128)S(1)}, f32[96,2,8,128]{3,2,1,0:T(8,128)S(1)}, f32[96,3,8,128]{3,2,1,0:T(8,128)S(1)}) custom-call(s32[132]{0:T(256)S(1)} %select_reduce_fusion.src_ref, s32[128]{0:T(128)S(1)} %bitcast_select_fusion.lane_ref, s32[192]{0:T(256)S(1)} %fusion.2.row_ref, s32[8,128]{1,0:T(8,128)S(1)} %pad.4.beside_ref, ...), custom_call_target="tpu_custom_call" | custom-call | tf_op jit(solution)/shard_map/pallas_call | solution.py:552
  114.9 1.0 copy.16
  115.9 0.9 copy.17
  116.7 1.0 copy.18
  (5 shorter events, 0.1 us)
Async XLA Ops:
  3.2 1.1 copy-start
  4.3 1.1 copy-start.1
  5.5 1.1 copy-start.2
where the time goes:
time: 118 us
  Pallas kernels  108 us (92%)
  local copies, waits for them, and re-layouts  7.29 us (6%)
  other arithmetic  1.51 us (1%)
    pallas_call x1, Pallas kernels, on_device(): pl.pallas_call(functools.partial(kernel, owners, sectors), out_shape=(jax...  108 us
    unnamed x10, local copies, waits for them, and re-layouts  6.95 us

commit v1 on v0

v1 whole, which is shorter than its diff:
```python
import functools
import types

import jax
import jax.numpy as jnp
from jax import lax
from jax.experimental import pallas as pl
from jax.experimental.pallas import tpu as pltpu
from jax.sharding import PartitionSpec as P

SCOLS = 4
ITERS = 4
VMEM_MB = 56

strength_scale = 4.0
cover_decay = 4.0
elastic_weight = 1.0
ellipse_square = 4.0
delta_floor = 0.05
inertia = 2.0
speed_floor = 0.2
coriolis = 0.6

MESH = pl.DeviceIdType.MESH


SCRATCH = (
    "ocean_ref", "vel", "sig", "area_in", "thick_in", "ocean_acc", "send_buf", "edge_send",
    "forcing", "edge_land", "cover", "area_buf", "mass_buf", "strength_buf", "blend", "back",
    "rows_0", "rows_1", "rows_i", "next_0", "next_1", "prev_0", "prev_1", "prev_i", "pick_next",
    "pick_prev", "first_rows", "ghost_flow", "ghost_row", "ghost_col", "upper", "corner",
    "local_sems", "out_send", "out_recv", "edge_sems", "fwd_send", "fwd_recv", "cover_sems",
    "halo_send", "halo_recv", "ret_send", "ret_recv", "ret_edge", "back_send", "back_recv",
)


def stress_update(flow_x, flow_y, down_x, down_y, right_x, right_y, one, two, shear, strength):
    stretch_x = down_x - flow_x
    stretch_y = right_y - flow_y
    shear_rate = right_x - flow_x + (down_y - flow_y)
    divergence = stretch_x + stretch_y
    tension = stretch_x - stretch_y
    square = (
        divergence * divergence
        + (tension * tension + shear_rate * shear_rate) * (1.0 / ellipse_square)
        + delta_floor * delta_floor
    )
    weight = elastic_weight * strength * lax.rsqrt(square)
    relax = 1.0 / (1.0 + elastic_weight)
    return (
        (one + weight * divergence - elastic_weight * strength) * relax,
        (two + weight * tension * (1.0 / ellipse_square)) * relax,
        (shear + weight * shear_rate * (0.5 / ellipse_square)) * relax,
    )


def kernel(owners, sectors, *refs):
    (
        src_ref,
        lane_ref,
        row_ref,
        beside_ref,
        ocean_hbm,
        vel_hbm,
        stress_hbm,
        area_hbm,
        thick_hbm,
        ocean_out,
        vel_out,
        sig_out,
    ) = refs[:12]
    r = types.SimpleNamespace(**dict(zip(SCRATCH, refs[12:], strict=True)))
    group = lax.axis_index("groups")
    me = lax.axis_index("blk")
    sector = lax.axis_index("sub")
    lev = lax.axis_index("lev")
    ocean_ref, vel, sig, forcing, blend, back = (
        r.ocean_ref, r.vel, r.sig, r.forcing, r.blend, r.back
    )
    slots = vel.shape[0]
    blocks = ocean_ref.shape[0]
    cap = blocks // owners
    chunks = slots // cap
    half = slots // 2
    unit = 4 * half + 32
    f32 = jnp.float32

    def at(blk, sub=None, core=None):
        return (
            group,
            blk,
            sector if sub is None else sub,
            lev if core is None else core,
        )

    partner = at(me, None, 1 - lev)

    def remote(src, dst, send, recv, target):
        return pltpu.make_async_remote_copy(
            src_ref=src,
            dst_ref=dst,
            send_sem=send,
            recv_sem=recv,
            device_id=target,
            device_id_type=MESH,
        )

    local = [
        pltpu.make_async_copy(src, dst, r.local_sems.at[i])
        for i, (src, dst) in enumerate((
            (ocean_hbm, ocean_ref),
            (vel_hbm, vel),
            (area_hbm, r.area_in),
            (thick_hbm, r.thick_in),
            (stress_hbm, sig),
        ))
    ]
    for copy in local:
        copy.start()

    lanes = lax.broadcasted_iota(jnp.int32, (8, 128), 1)
    subs = lax.broadcasted_iota(jnp.int32, (8, 128), 0)
    zero = jnp.zeros((8, 128), f32)

    rows = (r.rows_0, r.rows_1)
    crossed_next = (r.next_0, r.next_1)
    crossed_prev = (r.prev_0, r.prev_1)
    for ref in (*rows, r.rows_i):
        for a in (2, 3):
            ref[a * unit + 4 * half : (a + 1) * unit, :] = jnp.zeros((32, 128), f32)
        rest = ref.shape[0] - 4 * unit
        ref[4 * unit :, :] = jnp.zeros((rest, 128), f32)
    for ref in (*crossed_next, *crossed_prev, r.prev_i):
        ref[...] = jnp.zeros(ref.shape, f32)

    barrier = pltpu.get_barrier_semaphore()

    def greet(target):
        pl.semaphore_signal(barrier, inc=1, device_id=target, device_id_type=MESH)

    greet(partner)
    for delta in range(1, owners):
        greet(at(lax.rem(me + delta, owners)))
    expected = owners
    for ds in (-1, 1):
        for da in (-1, 0, 1):
            q, o = sector + ds, me + da
            ok = (q >= 0) & (q < sectors) & (o >= 0) & (o < owners)

            @pl.when(ok)
            def _():
                greet(at(o, q))

            expected = expected + ok.astype(jnp.int32)
    local[0].wait()
    pl.semaphore_wait(barrier, expected)

    def out_copy(o, s):
        return remote(
            r.send_buf.at[o],
            forcing.at[lev, pl.ds(s * cap, cap)],
            r.out_send.at[o],
            r.out_recv.at[s],
            at(o),
        )

    full = me * cap < slots

    def take(lane, fields):
        src = src_ref[lane]
        safe = jnp.maximum(src, 0)
        return [jnp.where(src >= 0, ocean_ref[safe, f], 0.0) for f in fields]

    for delta in range(1, owners):
        o = lax.rem(me + delta, owners)

        @pl.when(full)
        def _():
            def fill(g, c):
                tiles = [take(o * cap + 4 * g + i, (2 * lev, 2 * lev + 1)) for i in range(4)]
                for i in range(4):
                    for f in range(2):
                        r.send_buf[o, 4 * g + i, f] = tiles[i][f]
                return c

            lax.fori_loop(0, cap // 4, fill, 0)
            out_copy(o, me).start()

    def edge_owner(s):
        last_pass = s * (cap // SCOLS) - 1
        return jnp.where(lax.rem(last_pass + 2, 2) == 0, owners - 1, 0)

    def has_edge(s):
        return (s >= 1) & (s <= chunks)

    def edge_copy(s, o):
        return remote(
            r.edge_send, r.edge_land.at[s], r.edge_sems.at[0], r.edge_sems.at[1 + s], at(o)
        )

    @pl.when(has_edge(me))
    def _():
        for j in range(SCOLS):
            tiles = take(blocks + j, range(4))
            for f in range(4):
                r.edge_send[j, f] = tiles[f]
        edge_copy(me, edge_owner(me)).start()

    def line_copies(ref, base):
        return [
            (me + 1 < owners, remote(
                ref.at[pl.ds(0, unit)], ref.at[pl.ds(2 * unit, unit)],
                r.halo_send.at[base], r.halo_recv.at[base], at(me + 1)), me >= 1),
            (me >= 1, remote(
                ref.at[pl.ds(unit, unit)], ref.at[pl.ds(3 * unit, unit)],
                r.halo_send.at[base + 1], r.halo_recv.at[base + 1], at(me - 1)),
                me + 1 < owners),
        ]

    def cross_copies(cols, cross, down, base):
        target, source = sector + down, sector - down
        t_ok = (target >= 0) & (target < sectors)
        s_ok = (source >= 0) & (source < sectors)
        made = []
        for i, da in enumerate((1, 0, -1)):
            o, p = me + da, me - da
            made.append((t_ok & (o >= 0) & (o < owners), remote(
                cols, cross.at[1 - da], r.halo_send.at[base + i], r.halo_recv.at[base + i],
                at(o, target)), s_ok & (p >= 0) & (p < owners)))
        return made

    def halo_copies(parity):
        ref, base = rows[parity], 8 * parity
        first = ref.at[pl.ds(4 * half, 16)]
        last = ref.at[pl.ds(4 * half + 16, 16)]
        return (
            cross_copies(first, crossed_next[parity], -1, base + 2)
            + cross_copies(last, crossed_prev[parity], 1, base + 5)
            + line_copies(ref, base)
        )

    halos = [halo_copies(0), halo_copies(1)]
    start_halo = cross_copies(
        r.rows_i.at[pl.ds(4 * half, 32)], r.prev_i, 1, 18
    ) + line_copies(r.rows_i, 16)

    def halo_start(copies):
        for ok, copy, _ in copies:
            pl.when(ok)(copy.start)

    def halo_wait(copies):
        for ok, copy, arriving in copies:
            pl.when(arriving)(copy.wait_recv)
            pl.when(ok)(copy.wait_send)

    def put_cols(ref, cols):
        for i, col in enumerate(cols):
            for a in range(2):
                low = a * unit + 4 * half + 8 * i
                ref[low : low + 8, :] = col

    def pack_flow(ref, g, flows, cols):
        cols = list(cols)
        for i, (x, y) in enumerate(flows):
            odd, pos = i // 4, 4 * g + i % 4
            first = 2 * half if odd else unit
            last = unit + 2 * half if odd else 0
            for f, tile in enumerate((x, y)):
                ref[pl.ds(first + f * half + pos, 1), :] = tile[0:1]
                ref[pl.ds(last + f * half + pos, 1), :] = tile[7:8]
                r.first_rows[f, pl.ds(8 * g + i, 1), :] = tile[0:1]
            here = lanes == 8 * g + i
            for f, tile in enumerate((x, y)):
                cols[f] = jnp.where(here, tile[:, 0:1], cols[f])
                cols[2 + f] = jnp.where(here, tile[:, 127:128], cols[2 + f])
        return tuple(cols)

    def start_body(g, cols):
        flows = [(vel[8 * g + i, 0], vel[8 * g + i, 1]) for i in range(8)]
        return pack_flow(rows[0], g, flows, cols)

    local[1].wait()
    cols = lax.fori_loop(0, slots // 8, start_body, (zero,) * 4)
    put_cols(rows[0], cols)
    halo_start(halos[0])

    local[2].wait()
    local[3].wait()

    def part_body(g, c):
        made = []
        for i in range(4):
            j = 4 * g + i
            first, second = r.area_in[j, 0], r.area_in[j, 1]
            made.append((
                first + second,
                first * r.thick_in[j, 0] + second * r.thick_in[j, 1],
            ))
        for i in range(4):
            r.cover[0, 0, 4 * g + i] = made[i][0]
            r.cover[0, 1, 4 * g + i] = made[i][1]
        return c

    lax.fori_loop(0, slots // 4, part_body, 0)
    cover_copy = remote(
        r.cover.at[0], r.cover.at[1], r.cover_sems.at[0], r.cover_sems.at[1], partner
    )
    cover_copy.start()

    @pl.when(full)
    def _():
        def fill(g, c):
            tiles = [take(me * cap + 2 * g + i, range(4)) for i in range(2)]
            for i in range(2):
                for f in range(4):
                    forcing[f // 2, me * cap + 2 * g + i, f % 2] = tiles[i][f]
            return c

        lax.fori_loop(0, cap // 2, fill, 0)

    spot = lax.broadcasted_iota(jnp.int32, (128, 128), 0)
    for pick, d, toward, low in (
        (r.pick_next, 1, 1, 0),
        (r.pick_next, 4, 1, 128),
        (r.pick_prev, 3, -1, 0),
        (r.pick_prev, 5, -1, 128),
    ):
        ids = beside_ref[d : d + 1, :]
        for i in range(6):
            across, aside = i % 3 - 1, (i // 3) * toward
            base = ((me + across) * sectors + sector + aside) * slots
            hit = (ids - base == spot) & (spot < slots) & (ids >= 0)
            pick[i * 128 : (i + 1) * 128, low : low + 128] = hit.astype(f32).astype(jnp.bfloat16)

    def fetch_columns(ref, low, count, cross, pick):
        parts = [
            ref[a * unit + 4 * half + low : a * unit + 4 * half + low + count, :]
            for a in (2, 0, 3)
        ] + [cross[a] for a in range(3)]
        whole = jnp.concatenate(parts, axis=1)
        first = whole.astype(jnp.bfloat16)
        rest = whole - first.astype(f32)
        second = rest.astype(jnp.bfloat16)
        third = (rest - second.astype(f32)).astype(jnp.bfloat16)
        terms = jnp.concatenate([first, second, third], axis=0)
        got = jnp.dot(terms, pick[...], preferred_element_type=f32)
        return got[0:count] + got[count : 2 * count] + got[2 * count : 3 * count]

    local[4].wait()
    cover_copy.wait()

    def cover_body(g, cols):
        cols = list(cols)
        for part in range(2):
            made = []
            for i in range(4):
                j = 8 * g + 4 * part + i
                area = r.cover[0, 0, j] + r.cover[1, 0, j]
                volume = r.cover[0, 1, j] + r.cover[1, 1, j]
                strength = strength_scale * volume * jnp.exp(-cover_decay * (1.0 - area))
                made.append((area, volume, strength, [sig[j, f] for f in range(3)] + [strength]))
            for i, (area, volume, strength, fields) in enumerate(made):
                j = 8 * g + 4 * part + i
                r.area_buf[j] = area
                r.mass_buf[j] = volume
                r.strength_buf[j] = strength
                for f, tile in enumerate(fields):
                    r.rows_i[pl.ds(part * unit + f * half + 4 * g + i, 1), :] = tile[7:8]
                    cols[f] = jnp.where(lanes == j, tile[:, 127:128], cols[f])
        return tuple(cols)

    cols = lax.fori_loop(0, slots // 8, cover_body, (zero,) * 4)
    put_cols(r.rows_i, cols)
    halo_start(start_halo)

    def fwd_copy(s, part):
        place = forcing.at[part, pl.ds(s * cap, cap)]
        return remote(place, place, r.fwd_send.at[s], r.fwd_recv.at[s], partner)

    def ret_copy(s, o):
        return remote(
            blend.at[lev, pl.ds(s * cap, cap)],
            back.at[lev, pl.ds(o * cap, cap)],
            r.ret_send.at[s],
            r.ret_recv.at[o],
            at(s),
        )

    def ret_edge_copy(s):
        return remote(
            blend.at[:, pl.ds(s * cap - SCOLS, SCOLS)],
            back.at[:, pl.ds(blocks, SCOLS)],
            r.ret_edge.at[1 + s],
            r.ret_edge.at[0],
            at(s),
        )

    sig_copy = pltpu.make_async_copy(sig, sig_out, r.local_sems.at[4])
    vel_copy = pltpu.make_async_copy(vel, vel_out, r.local_sems.at[1])

    for sweep in range(ITERS):
        parity = sweep % 2
        ref = rows[parity]
        final = sweep == ITERS - 1
        halo_wait(halos[parity])
        got = fetch_columns(ref, 0, 16, crossed_next[parity], r.pick_next)
        right_x, right_y = got[0:8, 0:128], got[8:16, 0:128]
        r.corner[...] = jnp.transpose(
            jnp.concatenate([got[:, 128:256], jnp.zeros((112, 128), f32)], axis=0)
        )
        got = fetch_columns(ref, 16, 16, crossed_prev[parity], r.pick_prev)
        left_x, left_y = got[0:8, 0:128], got[8:16, 0:128]
        under_x, under_y = got[0:1, 128:256], got[8:9, 128:256]

        def stress_body(g, c):
            for part in range(2):
                js = [8 * g + 4 * part + i for i in range(4)]
                last_row, last_col = subs == 7, lanes == 127
                made = []
                for j in js:
                    x, y = vel[j, 0], vel[j, 1]
                    place = row_ref[j]
                    above = row_ref[slots + j]
                    below_x = ref[pl.ds(place, 1), :]
                    below_y = ref[pl.ds(place + half, 1), :]
                    above_x = ref[pl.ds(above, 1), :]
                    above_y = ref[pl.ds(above + half, 1), :]
                    turn = 127 - j
                    new = stress_update(
                        x,
                        y,
                        jnp.where(last_row, below_x, pltpu.roll(x, 7, 0)),
                        jnp.where(last_row, below_y, pltpu.roll(y, 7, 0)),
                        jnp.where(last_col, pltpu.roll(right_x, turn, 1), pltpu.roll(x, 127, 1)),
                        jnp.where(last_col, pltpu.roll(right_y, turn, 1), pltpu.roll(y, 127, 1)),
                        sig[j, 0],
                        sig[j, 1],
                        sig[j, 2],
                        r.strength_buf[j],
                    )
                    made.append((new, above_x, above_y))
                for j, (new, above_x, above_y) in zip(js, made):
                    for f in range(3):
                        sig[j, f] = new[f]
                    r.ghost_flow[0, pl.ds(j, 1), :] = above_x
                    r.ghost_flow[1, pl.ds(j, 1), :] = above_y
            return c

        lax.fori_loop(0, slots // 8, stress_body, 0)
        if final:
            sig_copy.start()

        if sweep == 0:
            halo_wait(start_halo)

            def gather_body(g, c):
                for i in range(8):
                    j = 8 * g + i
                    place = row_ref[2 * slots + j]
                    for f in range(4):
                        r.ghost_row[f, pl.ds(j, 1), :] = r.rows_i[pl.ds(place + f * half, 1), :]
                return c

            lax.fori_loop(0, slots // 8, gather_body, 0)
            got = fetch_columns(r.rows_i, 0, 32, r.prev_i, r.pick_prev)
            for f in range(4):
                r.ghost_col[f] = got[8 * f : 8 * f + 8, 0:128]

        own_first = [
            ref[4 * half + 8 * f : 4 * half + 8 * f + 8, :] for f in range(2)
        ]
        new = stress_update(
            left_x,
            left_y,
            jnp.where(subs == 7, under_x, pltpu.roll(left_x, 7, 0)),
            jnp.where(subs == 7, under_y, pltpu.roll(left_y, 7, 0)),
            own_first[0],
            own_first[1],
            *[r.ghost_col[f] for f in range(4)],
        )
        for f in range(3):
            r.ghost_col[f] = new[f]
        left_shear = new[2]
        left_normal = 0.5 * (new[0] - new[1])

        def ghost_body(g, c):
            made = []
            for i in range(2):
                here = pl.ds(pl.multiple_of(16 * g + 8 * i, 8), 8)
                x, y = r.ghost_flow[0, here, :], r.ghost_flow[1, here, :]
                end = r.corner[here, :]
                new = stress_update(
                    x,
                    y,
                    r.first_rows[0, here, :],
                    r.first_rows[1, here, :],
                    jnp.where(lanes == 127, end[:, 7:8], pltpu.roll(x, 127, 1)),
                    jnp.where(lanes == 127, end[:, 15:16], pltpu.roll(y, 127, 1)),
                    *[r.ghost_row[f, here, :] for f in range(4)],
                )
                made.append((here, new))
            for here, new in made:
                for f in range(3):
                    r.ghost_row[f, here, :] = new[f]
                r.upper[0, here, :] = 0.5 * (new[0] + new[1])
                r.upper[1, here, :] = new[2]
            return c

        lax.fori_loop(0, slots // 16, ghost_body, 0)

        if sweep == 0:
            for s in range(chunks):

                @pl.when(me != s)
                def _():
                    out_copy(0, s).wait_recv()
                    fwd_copy(s, lev).start()

            for s in range(chunks):

                @pl.when(me != s)
                def _():
                    fwd_copy(s, 1 - lev).wait_recv()
                    fwd_copy(s, lev).wait_send()

            for s in range(1, chunks + 1):

                @pl.when(me == edge_owner(s))
                def _():
                    edge_copy(s, me).wait_recv()
                    for j in range(SCOLS):
                        for f in range(4):
                            spot_j = s * cap - SCOLS + j
                            forcing[f // 2, spot_j, f % 2] += r.edge_land[s, j, f]

        def flow_body(g, cols):
            here = pl.ds(pl.multiple_of(8 * g, 8), 8)
            upper_n, upper_s = r.upper[0, here, :], r.upper[1, here, :]
            flows = []
            first_row, first_col = subs == 0, lanes == 0
            for part in range(2):
                js = [8 * g + 4 * part + i for i in range(4)]
                made = []
                for i, j in enumerate(js):
                    k = 4 * part + i
                    x, y = vel[j, 0], vel[j, 1]
                    one, two, shear = sig[j, 0], sig[j, 1], sig[j, 2]
                    normal_x = 0.5 * (one + two)
                    normal_y = 0.5 * (one - two)
                    turn = jnp.where(j == 0, 0, 128 - j)
                    above_normal = jnp.where(
                        first_row, upper_n[k : k + 1], pltpu.roll(normal_x, 1, 0)
                    )
                    above_shear = jnp.where(
                        first_row, upper_s[k : k + 1], pltpu.roll(shear, 1, 0)
                    )
                    before_shear = jnp.where(
                        first_col, pltpu.roll(left_shear, turn, 1), pltpu.roll(shear, 1, 1)
                    )
                    before_normal = jnp.where(
                        first_col, pltpu.roll(left_normal, turn, 1), pltpu.roll(normal_y, 1, 1)
                    )
                    force_x = normal_x - above_normal + (shear - before_shear)
                    force_y = shear - above_shear + (normal_y - before_normal)
                    wind_x, wind_y = forcing[0, j, 0], forcing[0, j, 1]
                    cur_x, cur_y = forcing[1, j, 0], forcing[1, j, 1]
                    slip_x, slip_y = cur_x - x, cur_y - y
                    drag = jnp.sqrt(slip_x * slip_x + slip_y * slip_y + speed_floor * speed_floor)
                    mass = r.mass_buf[j]
                    heavy = mass * inertia
                    diagonal = heavy + drag
                    rotation = mass * coriolis
                    rhs_x = heavy * x + force_x + wind_x + drag * cur_x
                    rhs_y = heavy * y + force_y + wind_y + drag * cur_y
                    inverse = 1.0 / (diagonal * diagonal + rotation * rotation)
                    x = (diagonal * rhs_x + rotation * rhs_y) * inverse
                    y = (diagonal * rhs_y - rotation * rhs_x) * inverse
                    share = None
                    if final:
                        slip_x, slip_y = cur_x - x, cur_y - y
                        drag = jnp.sqrt(
                            slip_x * slip_x + slip_y * slip_y + speed_floor * speed_floor
                        )
                        area = r.area_buf[j]
                        share = (
                            area * drag * slip_x + (1.0 - area) * wind_x,
                            area * drag * slip_y + (1.0 - area) * wind_y,
                        )
                    made.append((x, y, share))
                for j, (x, y, share) in zip(js, made):
                    vel[j, 0] = x
                    vel[j, 1] = y
                    flows.append((x, y))
                    if final:
                        blend[0, j] = share[0]
                        blend[1, j] = share[1]
            if final:
                return cols
            return pack_flow(rows[1 - parity], g, flows, cols)

        if final:
            step = max(cap, 8)
            for low in range(0, slots, step):
                lax.fori_loop(low // 8, (low + step) // 8, flow_body, 0)
                for s in range(low // cap, (low + step) // cap):

                    @pl.when(me != s)
                    def _():
                        ret_copy(s, me).start()

            for s in range(1, chunks + 1):

                @pl.when(me == edge_owner(s))
                def _():
                    ret_edge_copy(s).start()

            vel_copy.start()
        else:
            cols = lax.fori_loop(0, slots // 8, flow_body, (zero,) * 4)
            put_cols(rows[1 - parity], cols)
            halo_start(halos[1 - parity])

    @pl.when(full)
    def _():
        def keep(g, c):
            tiles = [[blend[f, me * cap + 4 * g + i] for f in range(2)] for i in range(4)]
            for i in range(4):
                for f in range(2):
                    back[f, me * cap + 4 * g + i] = tiles[i][f]
            return c

        lax.fori_loop(0, cap // 4, keep, 0)

    def back_copy(o, part):
        place = back.at[part, pl.ds(o * cap, cap)]
        return remote(place, place, r.back_send.at[o], r.back_recv.at[o], partner)

    @pl.when(full)
    def _():
        for delta in range(1, owners):
            o = lax.rem(me + delta, owners)
            ret_copy(0, o).wait_recv()
            back_copy(o, lev).start()
        for delta in range(1, owners):
            o = lax.rem(me + delta, owners)
            back_copy(o, 1 - lev).wait_recv()
            back_copy(o, lev).wait_send()

    @pl.when(has_edge(me))
    def _():
        ret_edge_copy(me).wait_recv()
        edge_copy(me, edge_owner(me)).wait_send()

    def ocean_body(g, c):
        made = []
        for i in range(4):
            b = 4 * g + i
            lane = lane_ref[b]
            safe = jnp.maximum(lane, 0)
            made.append([
                jnp.where(lane >= 0, back[f, safe], ocean_ref[b, f]) for f in range(2)
            ])
        for i in range(4):
            for f in range(2):
                r.ocean_acc[4 * g + i, f] = made[i][f]
        return c

    lax.fori_loop(0, blocks // 4, ocean_body, 0)
    ocean_copy = pltpu.make_async_copy(r.ocean_acc, ocean_out, r.local_sems.at[0])
    ocean_copy.start()

    @pl.when(full)
    def _():
        for delta in range(1, owners):
            out_copy(lax.rem(me + delta, owners), me).wait_send()

    for s in range(chunks):

        @pl.when(me != s)
        def _():
            ret_copy(s, me).wait_send()

    for s in range(1, chunks + 1):

        @pl.when(me == edge_owner(s))
        def _():
            ret_edge_copy(s).wait_send()

    sig_copy.wait()
    vel_copy.wait()
    ocean_copy.wait()


def on_device(ocean_forcing, ice_home, ice_velocity, ice_stress, ice_area, ice_thick, neighbors):
    owners = lax.axis_size("blk")
    sectors = lax.axis_size("sub")
    me = lax.axis_index("blk")
    home = ice_home[0]
    blocks = ocean_forcing.shape[1]
    slots = ice_velocity.shape[1]
    cap = blocks // owners
    chunks = slots // cap
    half = slots // 2
    unit = 4 * half + 32

    position = lax.rem(home, slots) - me * cap
    lane = jnp.where(
        position >= 0, lax.div(home, slots) * cap + position, blocks + SCOLS + position
    )
    lane = jnp.where(home >= 0, lane, -1)
    wanted = jnp.arange(blocks + SCOLS, dtype=jnp.int32)
    ids = jnp.arange(blocks, dtype=jnp.int32)
    src = jnp.max(jnp.where(wanted[:, None] == lane[None, :], ids[None, :], -1), axis=1)

    beside = neighbors[0].T

    def places(ids, own_even, own_odd, prev, following):
        across = lax.div(ids, slots * sectors) - me
        slot = lax.rem(ids, slots)
        turn = lax.div(slot, SCOLS)
        pos = lax.div(turn, 2) * SCOLS + lax.rem(slot, SCOLS)
        own = jnp.where(lax.rem(turn, 2) == 1, own_odd, own_even)
        start = jnp.where(across == 0, own, jnp.where(across < 0, prev, following))
        return jnp.where(ids >= 0, jnp.clip(start + pos, 0, 4 * unit), 4 * unit)

    rows_at = jnp.concatenate([
        places(beside[0], unit, 2 * half, 2 * unit + 2 * half, 3 * unit),
        places(beside[2], 0, unit + 2 * half, 2 * unit, 3 * unit + 2 * half),
        places(beside[2], 0, unit, 2 * unit, 3 * unit),
    ])
    beside = jnp.pad(beside, ((0, 2), (0, 128 - slots)), constant_values=-1)

    f32 = jnp.float32
    tile = ocean_forcing.shape[3:]
    vmem = pl.BlockSpec(memory_space=pltpu.VMEM)
    smem = pl.BlockSpec(memory_space=pltpu.SMEM)
    anywhere = pl.BlockSpec(memory_space=pl.ANY)
    dma = pltpu.SemaphoreType.DMA

    def tiles(*lead):
        return pltpu.VMEM(lead + tile, f32)

    lines = 4 * unit + 3 * half + 8
    scratch = dict(
        ocean_ref=tiles(blocks, 4),
        vel=tiles(slots, 2),
        sig=tiles(slots, 3),
        area_in=tiles(slots, 2),
        thick_in=tiles(slots, 2),
        ocean_acc=tiles(blocks, 2),
        send_buf=tiles(owners, cap, 2),
        edge_send=tiles(SCOLS, 4),
        forcing=tiles(2, slots, 2),
        edge_land=tiles(chunks + 1, SCOLS, 4),
        cover=tiles(2, 2, slots),
        area_buf=tiles(slots),
        mass_buf=tiles(slots),
        strength_buf=tiles(slots),
        blend=tiles(2, slots),
        back=tiles(2, blocks + SCOLS),
        rows_0=pltpu.VMEM((lines, 128), f32),
        rows_1=pltpu.VMEM((lines, 128), f32),
        rows_i=pltpu.VMEM((lines, 128), f32),
        next_0=pltpu.VMEM((3, 16, 128), f32),
        next_1=pltpu.VMEM((3, 16, 128), f32),
        prev_0=pltpu.VMEM((3, 16, 128), f32),
        prev_1=pltpu.VMEM((3, 16, 128), f32),
        prev_i=pltpu.VMEM((3, 32, 128), f32),
        pick_next=pltpu.VMEM((6 * 128, 256), jnp.bfloat16),
        pick_prev=pltpu.VMEM((6 * 128, 256), jnp.bfloat16),
        first_rows=pltpu.VMEM((2, slots, 128), f32),
        ghost_flow=pltpu.VMEM((2, slots, 128), f32),
        ghost_row=pltpu.VMEM((4, slots, 128), f32),
        ghost_col=tiles(4),
        upper=pltpu.VMEM((2, slots, 128), f32),
        corner=pltpu.VMEM((128, 128), f32),
        local_sems=dma((5,)),
        out_send=dma((owners,)),
        out_recv=dma((owners,)),
        edge_sems=dma((chunks + 2,)),
        fwd_send=dma((chunks,)),
        fwd_recv=dma((chunks,)),
        cover_sems=dma((2,)),
        halo_send=dma((21,)),
        halo_recv=dma((21,)),
        ret_send=dma((chunks,)),
        ret_recv=dma((owners,)),
        ret_edge=dma((chunks + 2,)),
        back_send=dma((owners,)),
        back_recv=dma((owners,)),
    )
    outs = pl.pallas_call(
        functools.partial(kernel, owners, sectors),
        out_shape=(
            jax.ShapeDtypeStruct((blocks, 2) + tile, f32),
            jax.ShapeDtypeStruct((slots, 2) + tile, f32),
            jax.ShapeDtypeStruct((slots, 3) + tile, f32),
        ),
        in_specs=[smem] * 3 + [vmem] + [anywhere] * 5,
        out_specs=(anywhere,) * 3,
        scratch_shapes=[scratch[name] for name in SCRATCH],
        compiler_params=pltpu.CompilerParams(
            collective_id=0, has_side_effects=True, vmem_limit_bytes=VMEM_MB * 2**20
        ),
    )(
        src,
        lane,
        rows_at,
        beside,
        ocean_forcing[0],
        ice_velocity[0],
        ice_stress[0],
        ice_area[0],
        ice_thick[0],
    )
    return tuple(out[None] for out in outs)


def solution(mesh):
    return jax.shard_map(
        on_device,
        mesh=mesh,
        in_specs=(
            P(("groups", "sub"), "blk", None, None, None),
            P(("groups", "sub"), "blk"),
            P(("groups", "sub"), "blk", None, None, None),
            P(("groups", "sub"), "blk", None, None, None),
            P(("groups", "sub"), "blk", "lev", None, None),
            P(("groups", "sub"), "blk", "lev", None, None),
            P(("groups", "sub"), "blk", None),
        ),
        out_specs=(
            P(("groups", "sub"), "blk", None, None, None),
            P(("groups", "sub"), "blk", None, None, None),
            P(("groups", "sub"), "blk", None, None, None),
        ),
        check_vma=False,
    )
```

time: 118 us -> 88.2 us (0.75)
  Pallas kernels: 108 us -> 79.1 us
    pallas_call x1, Pallas kernels: 108 us -> 79.1 us  [on_device(): pl.pallas_call(functools.partial(kernel, owners, sectors), out_shape=(jax...]
    unnamed x10, local copies, waits for them, and re-layouts: 6.95 us -> 5.59 us
where the time goes in v1:
time: 88.2 us; the launch traced here: 88 us
  Pallas kernels  79.1 us (90%)
  local copies, waits for them, and re-layouts  6.19 us (7%)
  other arithmetic  2.06 us (2%)
    pallas_call x1, Pallas kernels, on_device(): pl.pallas_call(functools.partial(kernel, owners, sectors), out_shape=(jax...  79.1 us
    unnamed x10, local copies, waits for them, and re-layouts  5.59 us

profile of v1, /device:TPU:0, one launch (start us, length us, event | category | flops | bytes accessed | tf_op | source)
XLA Modules:
  0.0 88.0 jit_solution(8586000315037453866)
XLA Ops:
  0.6 0.7 fusion.4.refs_1_
  1.3 0.0 copy-start.2
  1.3 0.7 select_reduce_fusion.refs_0_
  2.0 0.7 copy.12
  2.7 0.6 pad.4.refs_3_
  3.3 0.7 pad_add_fusion.refs_2_
  4.0 0.0 copy-done.2
  4.0 79.1 %shard_map.94 = (f32[128,2,8,128]{3,2,1,0:T(8,128)}, f32[96,2,8,128]{3,2,1,0:T(8,128)}, f32[96,3,8,128]{3,2,1,0:T(8,128)}) custom-call(s32[132]{0:T(256)} %select_reduce_fusion.refs_0_, s32[128]{0:T(128)} %copy-done.2, s32[288]{0:T(512)} %pad_add_fusion.refs_2_, s32[8,128]{1,0:T(8,128)} %pad.4.refs_3_, f32[128,4,8,128]{3,2,1,0:T(8,128)} %bitcast.83, ...), custom_call_target="tpu_custom_call" | custom-call | tf_op jit(solution)/shard_map/pallas_call | solution.py:792
  83.0 0.0 copy-start.1
  83.1 2.3 %copy.16 = f32[1,128,2,8,128]{4,3,2,1,0:T(8,128)} copy(f32[1,128,2,8,128]{4,3,2,1,0:T(8,128)} %bitcast.86) | data formatting | bytes 2097152
  85.4 0.0 copy-done.1
  85.4 0.0 copy-start
  85.4 0.9 copy.17
  86.3 0.7 copy-done
  87.0 1.0 %copy.18 = f32[1,96,3,8,128]{4,3,2,1,0:T(8,128)} copy(f32[1,96,3,8,128]{4,3,2,1,0:T(8,128)S(1)} %bitcast.84) | data formatting | bytes 2359296
  (2 shorter events, 0.1 us)
Async XLA Ops:
  1.3 2.7 %copy-start.2 = (s32[128]{0:T(128)}, s32[128]{0:T(128)S(1)}, u32[]{:S(2)}) copy-start(s32[128]{0:T(128)S(1)} %fusion.4.refs_1_) | copy-start | bytes 1540
  83.0 2.3 %copy-start.1 = (f32[96,2,8,128]{3,2,1,0:T(8,128)S(1)}, f32[96,2,8,128]{3,2,1,0:T(8,128)}, u32[]{:S(2)}) copy-start(f32[96,2,8,128]{3,2,1,0:T(8,128)} %get-tuple-element.7) | copy-start | bytes 2359300
  85.4 1.6 %copy-start = (f32[96,3,8,128]{3,2,1,0:T(8,128)S(1)}, f32[96,3,8,128]{3,2,1,0:T(8,128)}, u32[]{:S(2)}) copy-start(f32[96,3,8,128]{3,2,1,0:T(8,128)} %get-tuple-element.8) | copy-start | bytes 3538948

commit v2 on v1

--- a/solution.py
+++ b/solution.py
@@ -82,6 +82,7 @@
     cap = blocks // owners
     chunks = slots // cap
     half = slots // 2
+    quarter = half // 2
     unit = 4 * half + 32
     f32 = jnp.float32
 
@@ -171,7 +172,7 @@
         safe = jnp.maximum(src, 0)
         return [jnp.where(src >= 0, ocean_ref[safe, f], 0.0) for f in fields]
 
-    for delta in range(1, owners):
+    def send_share(delta):
         o = lax.rem(me + delta, owners)
 
         @pl.when(full)
@@ -186,6 +187,8 @@
             lax.fori_loop(0, cap // 4, fill, 0)
             out_copy(o, me).start()
 
+    send_share(1)
+
     def edge_owner(s):
         last_pass = s * (cap // SCOLS) - 1
         return jnp.where(lax.rem(last_pass + 2, 2) == 0, owners - 1, 0)
@@ -206,13 +209,14 @@
                 r.edge_send[j, f] = tiles[f]
         edge_copy(me, edge_owner(me)).start()
 
-    def line_copies(ref, base):
+    def line_copies(ref, base, low=0, high=unit):
+        count = high - low
         return [
             (me + 1 < owners, remote(
-                ref.at[pl.ds(0, unit)], ref.at[pl.ds(2 * unit, unit)],
+                ref.at[pl.ds(low, count)], ref.at[pl.ds(2 * unit + low, count)],
                 r.halo_send.at[base], r.halo_recv.at[base], at(me + 1)), me >= 1),
             (me >= 1, remote(
-                ref.at[pl.ds(unit, unit)], ref.at[pl.ds(3 * unit, unit)],
+                ref.at[pl.ds(unit + low, count)], ref.at[pl.ds(3 * unit + low, count)],
                 r.halo_send.at[base + 1], r.halo_recv.at[base + 1], at(me - 1)),
                 me + 1 < owners),
         ]
@@ -230,27 +234,34 @@
         return made
 
     def halo_copies(parity):
-        ref, base = rows[parity], 8 * parity
+        ref, base = rows[parity], 10 * parity
         first = ref.at[pl.ds(4 * half, 16)]
         last = ref.at[pl.ds(4 * half + 16, 16)]
         return (
             cross_copies(first, crossed_next[parity], -1, base + 2)
             + cross_copies(last, crossed_prev[parity], 1, base + 5)
-            + line_copies(ref, base)
-        )
-
+            + line_copies(ref, base, 2 * half, unit)
+        )
+
+    def early_copies(parity):
+        return line_copies(rows[parity], 10 * parity + 8, 0, 2 * half)
+
+    early = [early_copies(0), early_copies(1)]
     halos = [halo_copies(0), halo_copies(1)]
     start_halo = cross_copies(
-        r.rows_i.at[pl.ds(4 * half, 32)], r.prev_i, 1, 18
-    ) + line_copies(r.rows_i, 16)
+        r.rows_i.at[pl.ds(4 * half, 32)], r.prev_i, 1, 22
+    ) + line_copies(r.rows_i, 20)
 
     def halo_start(copies):
         for ok, copy, _ in copies:
             pl.when(ok)(copy.start)
 
     def halo_wait(copies):
-        for ok, copy, arriving in copies:
+        for _, copy, arriving in copies:
             pl.when(arriving)(copy.wait_recv)
+
+    def halo_sent(copies):
+        for ok, copy, _ in copies:
             pl.when(ok)(copy.wait_send)
 
     def put_cols(ref, cols):
@@ -259,15 +270,15 @@
                 low = a * unit + 4 * half + 8 * i
                 ref[low : low + 8, :] = col
 
-    def pack_flow(ref, g, flows, cols):
+    def pack_flow(ref, high, g, flows, cols):
         cols = list(cols)
         for i, (x, y) in enumerate(flows):
-            odd, pos = i // 4, 4 * g + i % 4
-            first = 2 * half if odd else unit
-            last = unit + 2 * half if odd else 0
+            odd, pos = i // 4, 4 * g + 3 * quarter * high + i % 4
+            first = 2 * quarter if odd else unit
+            last = unit + 2 * quarter if odd else 0
             for f, tile in enumerate((x, y)):
-                ref[pl.ds(first + f * half + pos, 1), :] = tile[0:1]
-                ref[pl.ds(last + f * half + pos, 1), :] = tile[7:8]
+                ref[pl.ds(first + f * quarter + pos, 1), :] = tile[0:1]
+                ref[pl.ds(last + f * quarter + pos, 1), :] = tile[7:8]
                 r.first_rows[f, pl.ds(8 * g + i, 1), :] = tile[0:1]
             here = lanes == 8 * g + i
             for f, tile in enumerate((x, y)):
@@ -275,14 +286,23 @@
                 cols[2 + f] = jnp.where(here, tile[:, 127:128], cols[2 + f])
         return tuple(cols)
 
-    def start_body(g, cols):
+    def start_body(high, g, cols):
         flows = [(vel[8 * g + i, 0], vel[8 * g + i, 1]) for i in range(8)]
-        return pack_flow(rows[0], g, flows, cols)
+        return pack_flow(rows[0], high, g, flows, cols)
 
     local[1].wait()
-    cols = lax.fori_loop(0, slots // 8, start_body, (zero,) * 4)
+    cols = (zero,) * 4
+    turns = slots // 16
+    for high in range(2):
+        cols = lax.fori_loop(
+            high * turns, (high + 1) * turns, functools.partial(start_body, high), cols
+        )
+        if high == 0:
+            halo_start(early[0])
     put_cols(rows[0], cols)
     halo_start(halos[0])
+    for delta in range(2, owners):
+        send_share(delta)
 
     local[2].wait()
     local[3].wait()
@@ -402,6 +422,7 @@
         parity = sweep % 2
         ref = rows[parity]
         final = sweep == ITERS - 1
+        halo_wait(early[parity])
         halo_wait(halos[parity])
         got = fetch_columns(ref, 0, 16, crossed_next[parity], r.pick_next)
         right_x, right_y = got[0:8, 0:128], got[8:16, 0:128]
@@ -422,9 +443,9 @@
                     place = row_ref[j]
                     above = row_ref[slots + j]
                     below_x = ref[pl.ds(place, 1), :]
-                    below_y = ref[pl.ds(place + half, 1), :]
+                    below_y = ref[pl.ds(place + quarter, 1), :]
                     above_x = ref[pl.ds(above, 1), :]
-                    above_y = ref[pl.ds(above + half, 1), :]
+                    above_y = ref[pl.ds(above + quarter, 1), :]
                     turn = 127 - j
                     new = stress_update(
                         x,
@@ -452,6 +473,7 @@
 
         if sweep == 0:
             halo_wait(start_halo)
+            halo_sent(start_halo)
 
             def gather_body(g, c):
                 for i in range(8):
@@ -485,8 +507,8 @@
 
         def ghost_body(g, c):
             made = []
-            for i in range(2):
-                here = pl.ds(pl.multiple_of(16 * g + 8 * i, 8), 8)
+            for i in range(4):
+                here = pl.ds(pl.multiple_of(32 * g + 8 * i, 8), 8)
                 x, y = r.ghost_flow[0, here, :], r.ghost_flow[1, here, :]
                 end = r.corner[here, :]
                 new = stress_update(
@@ -506,7 +528,9 @@
                 r.upper[1, here, :] = new[2]
             return c
 
-        lax.fori_loop(0, slots // 16, ghost_body, 0)
+        lax.fori_loop(0, slots // 32, ghost_body, 0)
+        halo_sent(early[parity])
+        halo_sent(halos[parity])
 
         if sweep == 0:
             for s in range(chunks):
@@ -533,7 +557,7 @@
                             spot_j = s * cap - SCOLS + j
                             forcing[f // 2, spot_j, f % 2] += r.edge_land[s, j, f]
 
-        def flow_body(g, cols):
+        def flow_body(high, g, cols):
             here = pl.ds(pl.multiple_of(8 * g, 8), 8)
             upper_n, upper_s = r.upper[0, here, :], r.upper[1, here, :]
             flows = []
@@ -596,12 +620,14 @@
                         blend[1, j] = share[1]
             if final:
                 return cols
-            return pack_flow(rows[1 - parity], g, flows, cols)
+            return pack_flow(rows[1 - parity], high, g, flows, cols)
 
         if final:
             step = max(cap, 8)
             for low in range(0, slots, step):
-                lax.fori_loop(low // 8, (low + step) // 8, flow_body, 0)
+                lax.fori_loop(
+                    low // 8, (low + step) // 8, functools.partial(flow_body, 0), 0
+                )
                 for s in range(low // cap, (low + step) // cap):
 
                     @pl.when(me != s)
@@ -616,7 +642,13 @@
 
             vel_copy.start()
         else:
-            cols = lax.fori_loop(0, slots // 8, flow_body, (zero,) * 4)
+            cols = (zero,) * 4
+            for high in range(2):
+                cols = lax.fori_loop(
+                    high * turns, (high + 1) * turns, functools.partial(flow_body, high), cols
+                )
+                if high == 0:
+                    halo_start(early[1 - parity])
             put_cols(rows[1 - parity], cols)
             halo_start(halos[1 - parity])
 
@@ -701,6 +733,7 @@
     cap = blocks // owners
     chunks = slots // cap
     half = slots // 2
+    quarter = half // 2
     unit = 4 * half + 32
 
     position = lax.rem(home, slots) - me * cap
@@ -714,19 +747,24 @@
 
     beside = neighbors[0].T
 
-    def places(ids, own_even, own_odd, prev, following):
+    def places(ids, skip, own_even, own_odd, prev, following):
         across = lax.div(ids, slots * sectors) - me
         slot = lax.rem(ids, slots)
         turn = lax.div(slot, SCOLS)
         pos = lax.div(turn, 2) * SCOLS + lax.rem(slot, SCOLS)
+        pos = pos + jnp.where(pos >= quarter, skip, 0)
         own = jnp.where(lax.rem(turn, 2) == 1, own_odd, own_even)
         start = jnp.where(across == 0, own, jnp.where(across < 0, prev, following))
         return jnp.where(ids >= 0, jnp.clip(start + pos, 0, 4 * unit), 4 * unit)
 
     rows_at = jnp.concatenate([
-        places(beside[0], unit, 2 * half, 2 * unit + 2 * half, 3 * unit),
-        places(beside[2], 0, unit + 2 * half, 2 * unit, 3 * unit + 2 * half),
-        places(beside[2], 0, unit, 2 * unit, 3 * unit),
+        places(
+            beside[0], 3 * quarter, unit, 2 * quarter, 2 * unit + 2 * quarter, 3 * unit
+        ),
+        places(
+            beside[2], 3 * quarter, 0, unit + 2 * quarter, 2 * unit, 3 * unit + 2 * quarter
+        ),
+        places(beside[2], 0, 0, unit, 2 * unit, 3 * unit),
     ])
     beside = jnp.pad(beside, ((0, 2), (0, 128 - slots)), constant_values=-1)
 
@@ -781,8 +819,8 @@
         fwd_send=dma((chunks,)),
         fwd_recv=dma((chunks,)),
         cover_sems=dma((2,)),
-        halo_send=dma((21,)),
-        halo_recv=dma((21,)),
+        halo_send=dma((25,)),
+        halo_recv=dma((25,)),
         ret_send=dma((chunks,)),
         ret_recv=dma((owners,)),
         ret_edge=dma((chunks + 2,)),

time: 88.2 us -> 85.4 us (0.968)
  Pallas kernels: 79.1 us -> 76.2 us
    pallas_call x1, Pallas kernels: 79.1 us -> 76.2 us  [on_device(): pl.pallas_call(functools.partial(kernel, owners, sectors), out_shape=(jax...]
where the time goes in v2:
time: 85.4 us; the launch traced here: 85.1 us
  Pallas kernels  76.2 us (89%)
  local copies, waits for them, and re-layouts  6.19 us (7%)
  other arithmetic  2.06 us (2%)
    pallas_call x1, Pallas kernels, on_device(): pl.pallas_call(functools.partial(kernel, owners, sectors), out_shape=(jax...  76.2 us
    unnamed x10, local copies, waits for them, and re-layouts  5.59 us

profile of v2, /device:TPU:0, one launch (start us, length us, event | category | flops | bytes accessed | tf_op | source)
XLA Modules:
  0.0 85.1 jit_solution(12985758474834837883)
XLA Ops:
  0.6 0.7 fusion.8.refs_1_
  1.3 0.0 copy-start.2
  1.3 0.7 select_reduce_fusion.refs_0_
  2.0 0.7 copy.12
  2.7 0.6 pad.4.refs_3_
  3.3 0.7 pad_add_fusion.refs_2_
  4.0 0.0 copy-done.2
  4.0 76.2 %shard_map.94 = (f32[128,2,8,128]{3,2,1,0:T(8,128)}, f32[96,2,8,128]{3,2,1,0:T(8,128)}, f32[96,3,8,128]{3,2,1,0:T(8,128)}) custom-call(s32[132]{0:T(256)} %select_reduce_fusion.refs_0_, s32[128]{0:T(128)} %copy-done.2, s32[288]{0:T(512)} %pad_add_fusion.refs_2_, s32[8,128]{1,0:T(8,128)} %pad.4.refs_3_, f32[128,4,8,128]{3,2,1,0:T(8,128)} %bitcast.83, ...), custom_call_target="tpu_custom_call" | custom-call | tf_op jit(solution)/shard_map/pallas_call | solution.py:830
  80.2 0.0 copy-start.1
  80.2 2.3 %copy.16 = f32[1,128,2,8,128]{4,3,2,1,0:T(8,128)} copy(f32[1,128,2,8,128]{4,3,2,1,0:T(8,128)} %bitcast.86) | data formatting | bytes 2097152
  82.6 0.0 copy-done.1
  82.6 0.0 copy-start
  82.6 0.9 %copy.17 = f32[1,96,2,8,128]{4,3,2,1,0:T(8,128)} copy(f32[1,96,2,8,128]{4,3,2,1,0:T(8,128)S(1)} %bitcast.87) | data formatting | bytes 1572864
  83.5 0.7 copy-done
  84.1 1.0 %copy.18 = f32[1,96,3,8,128]{4,3,2,1,0:T(8,128)} copy(f32[1,96,3,8,128]{4,3,2,1,0:T(8,128)S(1)} %bitcast.84) | data formatting | bytes 2359296
  (2 shorter events, 0.1 us)
Async XLA Ops:
  1.3 2.7 %copy-start.2 = (s32[128]{0:T(128)}, s32[128]{0:T(128)S(1)}, u32[]{:S(2)}) copy-start(s32[128]{0:T(128)S(1)} %fusion.8.refs_1_) | copy-start | bytes 1540
  80.2 2.3 %copy-start.1 = (f32[96,2,8,128]{3,2,1,0:T(8,128)S(1)}, f32[96,2,8,128]{3,2,1,0:T(8,128)}, u32[]{:S(2)}) copy-start(f32[96,2,8,128]{3,2,1,0:T(8,128)} %get-tuple-element.7) | copy-start | bytes 2359300
  82.6 1.6 %copy-start = (f32[96,3,8,128]{3,2,1,0:T(8,128)S(1)}, f32[96,3,8,128]{3,2,1,0:T(8,128)}, u32[]{:S(2)}) copy-start(f32[96,3,8,128]{3,2,1,0:T(8,128)} %get-tuple-element.8) | copy-start | bytes 3538948

commit v3 on v2

--- a/solution.py
+++ b/solution.py
@@ -10,7 +10,7 @@
 
 SCOLS = 4
 ITERS = 4
-VMEM_MB = 56
+VMEM_MB = 60
 
 strength_scale = 4.0
 cover_decay = 4.0
@@ -338,7 +338,9 @@
 
         lax.fori_loop(0, cap // 2, fill, 0)
 
-    spot = lax.broadcasted_iota(jnp.int32, (128, 128), 0)
+    spot = lax.broadcasted_iota(jnp.int32, (128, slots), 0)
+    for pick in (r.pick_next, r.pick_prev):
+        pick[...] = jnp.zeros(pick.shape, jnp.bfloat16)
     for pick, d, toward, low in (
         (r.pick_next, 1, 1, 0),
         (r.pick_next, 4, 1, 128),
@@ -350,7 +352,7 @@
             across, aside = i % 3 - 1, (i // 3) * toward
             base = ((me + across) * sectors + sector + aside) * slots
             hit = (ids - base == spot) & (spot < slots) & (ids >= 0)
-            pick[i * 128 : (i + 1) * 128, low : low + 128] = hit.astype(f32).astype(jnp.bfloat16)
+            pick[i * 128 : (i + 1) * 128, low : low + slots] = hit.astype(f32).astype(jnp.bfloat16)
 
     def fetch_columns(ref, low, count, cross, pick):
         parts = [
@@ -766,7 +768,6 @@
         ),
         places(beside[2], 0, 0, unit, 2 * unit, 3 * unit),
     ])
-    beside = jnp.pad(beside, ((0, 2), (0, 128 - slots)), constant_values=-1)
 
     f32 = jnp.float32
     tile = ocean_forcing.shape[3:]

time: 85.4 us -> 84.8 us (level)
    unnamed x10 -> x12, local copies, waits for them, and re-layouts: 5.59 us -> 5.6 us
where the time goes in v3:
time: 84.8 us; the launch traced here: 84.6 us
  Pallas kernels  76.2 us (90%)
  local copies, waits for them, and re-layouts  5.6 us (7%)
  other arithmetic  2.06 us (2%)
    pallas_call x1, Pallas kernels, on_device(): pl.pallas_call(functools.partial(kernel, owners, sectors), out_shape=(jax...  76.2 us
    unnamed x12, local copies, waits for them, and re-layouts  5.6 us

profile of v3, /device:TPU:0, one launch (start us, length us, event | category | flops | bytes accessed | tf_op | source)
XLA Modules:
  0.0 84.6 jit_solution(15454698182548733780)
XLA Ops:
  0.6 0.7 fusion.8.refs_1_
  1.3 0.0 copy-start.3
  1.3 0.7 select_reduce_fusion.refs_0_
  2.0 0.7 copy.12
  2.7 0.0 copy-start.2
  2.7 0.7 pad_add_fusion.refs_2_
  3.4 0.0 copy-done.3
  3.4 0.0 copy-done.2
  3.4 76.2 %shard_map.94 = (f32[128,2,8,128]{3,2,1,0:T(8,128)}, f32[96,2,8,128]{3,2,1,0:T(8,128)}, f32[96,3,8,128]{3,2,1,0:T(8,128)}) custom-call(s32[132]{0:T(256)} %select_reduce_fusion.refs_0_, s32[128]{0:T(128)} %copy-done.3, s32[288]{0:T(512)} %pad_add_fusion.refs_2_, s32[6,96]{1,0:T(8,128)} %bitcast.93, f32[128,4,8,128]{3,2,1,0:T(8,128)} %bitcast.83, ...), custom_call_target="tpu_custom_call" | custom-call | tf_op jit(solution)/shard_map/pallas_call | solution.py:831
  79.6 0.0 copy-start.1
  79.6 2.3 %copy.16 = f32[1,128,2,8,128]{4,3,2,1,0:T(8,128)} copy(f32[1,128,2,8,128]{4,3,2,1,0:T(8,128)} %bitcast.86) | data formatting | bytes 2097152
  82.0 0.0 copy-done.1
  82.0 0.0 copy-start
  82.0 0.9 %copy.17 = f32[1,96,2,8,128]{4,3,2,1,0:T(8,128)} copy(f32[1,96,2,8,128]{4,3,2,1,0:T(8,128)S(1)} %bitcast.87) | data formatting | bytes 1572864
  82.9 0.7 copy-done
  83.5 1.0 %copy.18 = f32[1,96,3,8,128]{4,3,2,1,0:T(8,128)} copy(f32[1,96,3,8,128]{4,3,2,1,0:T(8,128)S(1)} %bitcast.84) | data formatting | bytes 2359296
  (2 shorter events, 0.1 us)
Async XLA Ops:
  1.3 2.1 %copy-start.3 = (s32[128]{0:T(128)}, s32[128]{0:T(128)S(1)}, u32[]{:S(2)}) copy-start(s32[128]{0:T(128)S(1)} %fusion.8.refs_1_) | copy-start | bytes 1540
  2.7 0.7 copy-start.2
  79.6 2.3 %copy-start.1 = (f32[96,2,8,128]{3,2,1,0:T(8,128)S(1)}, f32[96,2,8,128]{3,2,1,0:T(8,128)}, u32[]{:S(2)}) copy-start(f32[96,2,8,128]{3,2,1,0:T(8,128)} %get-tuple-element.7) | copy-start | bytes 2359300
  82.0 1.6 %copy-start = (f32[96,3,8,128]{3,2,1,0:T(8,128)S(1)}, f32[96,3,8,128]{3,2,1,0:T(8,128)}, u32[]{:S(2)}) copy-start(f32[96,3,8,128]{3,2,1,0:T(8,128)} %get-tuple-element.8) | copy-start | bytes 3538948
